TPU v7x, 32 devices: a whole 2x2x4 slice. The times are simulated.
32 devices in a mesh: pipe: 2 (over core), dp: 16 (over z, y, x).
Axes of the slice: x: 2, y: 2, z: 4, core: 2. Of those that a mesh axis runs over, the one named last changes fastest.
Arguments:
- images: bfloat16 [64, 24, 24, 320], P('dp'), may hold values from -6 to 6
- masks: int32 [64, 24, 24], P('dp'), may hold values from 0 to 1, as said below
- conv_weight: bfloat16 [2, 9, 320], P('pipe'), may hold values from -2 to 2
- batch_gain: float32 [2, 320], P('pipe'), may hold values from 0.5 to 1.5
- batch_bias: float32 [2, 320], P('pipe'), may hold values from -3 to 3
- width_weight: bfloat16 [2, 24, 24], P('pipe'), may hold values from -1.25 to 1.25
- width_bias: float32 [2, 24], P('pipe'), may hold values from -3 to 3
- height_weight: bfloat16 [2, 24, 24], P('pipe'), may hold values from -1.25 to 1.25
- height_bias: float32 [2, 24], P('pipe'), may hold values from -3 to 3
- merge_weight: bfloat16 [2, 960, 320], P('pipe'), may hold values from -0.1875 to 0.1875
- merge_bias: float32 [2, 320], P('pipe'), may hold values from -3 to 3
- norm_gain: float32 [2, 320], P('pipe'), may hold values from 0.5 to 1.5
- norm_bias: float32 [2, 320], P('pipe'), may hold values from -3 to 3
- up_weight: bfloat16 [2, 320, 1280], P('pipe'), may hold values from -0.3125 to 0.3125
- up_bias: float32 [2, 1280], P('pipe'), may hold values from -3 to 3
- down_weight: bfloat16 [2, 1280, 320], P('pipe'), may hold values from -0.25 to 0.25
- down_bias: float32 [2, 320], P('pipe'), may hold values from -3 to 3
- out_grad: bfloat16 [64, 24, 24, 320], P('dp'), may hold values from -6 to 6
Outputs:
- section_outputs: bfloat16 [2, 64, 24, 24, 320], P('pipe', 'dp')
- input_grads: bfloat16 [2, 64, 24, 24, 320], P('pipe', 'dp')
- conv_grad: float32 [2, 9, 320], P('pipe')
- batch_gain_grad: float32 [2, 320], P('pipe')
- batch_bias_grad: float32 [2, 320], P('pipe')
- width_grad: float32 [2, 24, 24], P('pipe')
- width_bias_grad: float32 [2, 24], P('pipe')
- height_grad: float32 [2, 24, 24], P('pipe')
- height_bias_grad: float32 [2, 24], P('pipe')
- merge_grad: float32 [2, 960, 320], P('pipe')
- merge_bias_grad: float32 [2, 320], P('pipe')
- norm_gain_grad: float32 [2, 320], P('pipe')
- norm_bias_grad: float32 [2, 320], P('pipe')
- up_grad: float32 [2, 320, 1280], P('pipe')
- up_bias_grad: float32 [2, 1280], P('pipe')
- down_grad: float32 [2, 1280, 320], P('pipe')
- down_bias_grad: float32 [2, 320], P('pipe')
Inputs may be any that keep to these rules, and one draw needn't show every extreme that they name: `masks`: each image's valid patches are its first h rows and first w columns, h and w between 8 and 24.
All inputs are finite; a program needn't handle non-finite values.
Results may differ from a plain program's by a relative error of at most 0.014.
Values may be sent and summed in bfloat16 or wider, within the bound.
A program may use at most 128 MiB of HBM per device.

v0:
```python
import functools

import jax
import jax.numpy as jnp
from jax import lax
from jax.experimental import pallas as pl
from jax.experimental.pallas import tpu as pltpu
from jax.sharding import PartitionSpec as P

EPS = 1e-05
MESH = pl.DeviceIdType.MESH
F32 = jnp.float32
BF16 = jnp.bfloat16

SIDE = 24
ROWS = SIDE * SIDE
C = 320
CP = 384
FF = 1280
FT = 256
CHUNK = 48
TILE = 32
LANES = ((0, 128), (128, 256), (256, 320))
GROUP = 8 * SIDE

HALF = C // 2
SHARD = HALF // 2
WIDE = FF // 2
SHARDS = 4
MT = 512
STEP = 8

CONV, BGAIN, BBIAS, MBIAS, NGAIN, NBIAS, DBIAS, WBIAS, HBIAS, UBIAS, WW, HW, PACK = (
    0, 16, 17, 18, 19, 20, 21, 22, 23, 24, 32, 56, 80)
SMALL = 16


def dot(a, b, contract=(1, 0), precision=None):
    return lax.dot_general(
        a, b, (((contract[0],), (contract[1],)), ((), ())),
        preferred_element_type=F32, precision=precision)


def fold(value):
    rows = value.shape[0]
    return jnp.sum(value.reshape(rows // 8, 8, value.shape[1]), 0)


def total(partial):
    return jnp.sum(partial, 0, keepdims=True)


def grid_row(index):
    return (index * 2731) >> 16


def one_hots(rows):
    place = lax.broadcasted_iota(jnp.int32, (rows, SIDE), 0)
    lane = lax.broadcasted_iota(jnp.int32, (rows, SIDE), 1)
    i = grid_row(place)
    return i == lane, place - SIDE * i == lane


def gelu_both(x):
    e = jnp.exp2(x * x * -0.7213475204444817)
    d = 1.0 + 0.23164189 * jnp.abs(x)
    t = pl.reciprocal(d, approx=True)
    t = t * (2.0 - d * t)
    poly = t * (0.127414796 + t * (-0.142248368 + t * (0.7107068705 + t * (-0.7265760135 + t * 0.5307027145))))
    tail = poly * e
    phi = jnp.where(x >= 0, 1.0 - tail, tail)
    return x * phi, phi + x * e * 0.3989422804014327


def kernel(
    n_dp,
    images, masks, conv_w, bgain, bbias, wwt, wb, hwt, hb, wm_h, mbias, ngain, nbias, wu_h, ubias, wd_h, dbias, og_h,
    so_h, ig_h, gd_h, gu_h, gm_h, gs_h, sp_hidden, sp_gp, sp_joined, sp_normal, sp_xl,
    mask_cols, stat, own_column, i_hot, pack, wm, wmid, wu, wd, ub, uf, cv, joined, normal, xl, rstd, hidden, gp,
    gf, gb, gmb, gwb, gbt, gpre, gmix, gwh, gsh, kw, kh, wbcol, hbcol,
    gw_acc, gh_acc, wcol, hcol, ybuf, msg, land, acc_d, acc_u, acc_m, gs,
    sb_d, lb_d, rl_d, sb_u, lb_u, rl_u, sb_m, lb_m, rl_m, small_land, conv_land,
    local_sems, again_sems, pack_sems, w_send, w_recv, st_send, st_recv,
    so_local, so_send, so_recv, ig_local, ig_send, ig_recv, spill_sems, fetch_sems,
    red_send, red_recv, small_send, small_recv, conv_send, conv_recv, out_local, out_send, out_recv, gs_sem,
):
    me_p = lax.axis_index("pipe")
    me_d = lax.axis_index("dp")
    other = 1 - me_p
    first = gsh.at[2, pl.ds(SIDE, ROWS)]
    igbuf = ybuf
    gnorm = gsh.at[0, pl.ds(SIDE, ROWS)]

    def image_copy(t, sems):
        return pltpu.make_async_copy(images.at[2 * me_p + t], ub.at[t], sems)

    image_in = [image_copy(t, local_sems.at[5 + t]) for t in range(2)]
    grad_in = [pltpu.make_async_copy(og_h.at[2 * me_p + t], ub.at[t], local_sems.at[7 + t]) for t in range(2)]
    weights = ((wm_h, wm), (wu_h, wu), (wd_h, wd))
    weights_in = [pltpu.make_async_copy(src, dst.at[me_p], local_sems.at[n]) for n, (src, dst) in enumerate(weights)]
    for copy in image_in + weights_in:
        copy.start()

    barrier = pltpu.get_barrier_semaphore()

    def greet(step, carry):
        pl.semaphore_signal(barrier, inc=1, device_id={"dp": lax.rem(me_d + step, n_dp)}, device_id_type=MESH)
        return carry

    lax.fori_loop(1, n_dp, greet, 0)
    pl.semaphore_signal(barrier, inc=1, device_id={"pipe": other}, device_id_type=MESH)

    pack[me_p] = jnp.zeros(pack.shape[1:], F32)
    pack[me_p, CONV : CONV + 9, :] = conv_w[0].astype(F32)
    for row, ref in ((BGAIN, bgain), (BBIAS, bbias), (MBIAS, mbias), (NGAIN, ngain), (NBIAS, nbias), (DBIAS, dbias)):
        pack[me_p, row : row + 1, :] = ref[...]
    for row, ref in ((WBIAS, wb), (HBIAS, hb)):
        pack[me_p, row : row + 1, 0:SIDE] = ref[...]
    for n in range(FF // FT):
        pack[me_p, UBIAS + n : UBIAS + n + 1, 0:FT] = ubias[:, n * FT : n * FT + FT]
    for row, ref in ((WW, wwt), (HW, hwt)):
        pack[me_p, row : row + SIDE, 0:SIDE] = ref[0].astype(F32)

    pl.semaphore_wait(barrier, n_dp)

    def across(src, dst, send, recv):
        return pltpu.make_async_remote_copy(
            src_ref=src, dst_ref=dst, send_sem=send, recv_sem=recv,
            device_id={"pipe": other}, device_id_type=MESH)

    pack_over = across(pack.at[me_p], pack.at[me_p], pack_sems.at[0], pack_sems.at[1])
    weights_over = [across(src, dst.at[me_p], w_send.at[n], w_recv.at[n]) for n, (src, dst) in enumerate(weights)]
    pack_over.start()
    for copy in weights_over:
        copy.start()

    msg[...] = jnp.zeros(msg.shape, F32)
    for k in range(2):
        for acc in (acc_d, acc_u, acc_m):
            for n in range(2):
                acc[k, n] = jnp.zeros(acc.shape[2:], F32)
        gs[k] = jnp.zeros(gs.shape[1:], F32)
    for n in range(2):
        uf[n, 0:SIDE, :] = jnp.zeros((SIDE, C), F32)
        uf[n, SIDE + ROWS : 2 * SIDE + ROWS, :] = jnp.zeros((SIDE, C), F32)
    for n in range(3):
        gsh[n, 0:SIDE, :] = jnp.zeros((SIDE, C), F32)
        gsh[n, SIDE + ROWS : 2 * SIDE + ROWS, :] = jnp.zeros((SIDE, C), F32)

    i_r, j_r = one_hots(ROWS)
    i_hot[...] = jnp.where(i_r, 1.0, 0.0).astype(BF16)
    q = lax.broadcasted_iota(jnp.int32, (SIDE, ROWS), 1)
    q = q - SIDE * grid_row(q)
    own_column[...] = jnp.where(lax.broadcasted_iota(jnp.int32, (SIDE, ROWS), 0) == q, 1.0, 0.0)
    for t in range(2):
        chosen = dot(i_hot[...], masks[2 * me_p + t].astype(F32).astype(BF16))
        mask_cols[t] = jnp.sum(jnp.where(j_r, chosen, 0.0), 1, keepdims=True)

    def later(value):
        at = lax.broadcasted_iota(jnp.int32, value.shape, 0)
        return jnp.where(at != 0, pltpu.roll(value, 1, 0), 0.0)

    def sooner(value):
        at = lax.broadcasted_iota(jnp.int32, value.shape, 0)
        return jnp.where(at != SIDE - 1, pltpu.roll(value, SIDE - 1, 0), 0.0)

    def grid_rows(body, init):
        def step(c, carry):
            for row in range(STEP):
                carry = body(pl.multiple_of(c * (STEP * SIDE), STEP * SIDE) + row * SIDE, carry)
            return carry
        return lax.fori_loop(0, SIDE // STEP, step, init)

    def groups(body, init):
        for g in range(ROWS // GROUP):
            init = body(g * GROUP, init)
        return init

    def send_stats(r):
        def one(step, carry):
            pltpu.make_async_remote_copy(
                src_ref=msg.at[r], dst_ref=land.at[r, n_dp - 1 - step],
                send_sem=st_send.at[r], recv_sem=st_recv.at[r],
                device_id={"dp": lax.rem(me_d + step, n_dp)}, device_id_type=MESH).start()
            return carry
        lax.fori_loop(1, n_dp, one, 0)

    def wait_stats(r):
        whole = pltpu.make_async_remote_copy(
            src_ref=land.at[r], dst_ref=land.at[r], send_sem=st_send.at[r], recv_sem=st_recv.at[r],
            device_id={"dp": lax.rem(me_d + 1, n_dp)}, device_id_type=MESH)
        whole.wait_send()
        whole.wait_recv()

    def conv_stage(t, k):
        z = 2 * k + t
        n_own = total(mask_cols[t])
        taps = [[pack[k, CONV + n : CONV + n + 1, l:m] for n in range(9)] for l, m in LANES]

        def conv(start, acc):
            at = pl.ds(start, SIDE)
            new = []
            for (l, m), tap, one in zip(LANES, taps, acc):
                rows = [uf[t, pl.ds(start + SIDE * r, SIDE), l:m] for r in range(3)]
                part = [rows[0] * tap[s] + rows[1] * tap[3 + s] + rows[2] * tap[6 + s] for s in range(3)]
                out = part[1] + later(part[0]) + sooner(part[2])
                cv[z, at, l:m] = out
                new.append(one + fold(out * mask_cols[t, at, :]))
            return new
        acc = grid_rows(conv, [jnp.zeros((8, m - l), F32) for l, m in LANES])
        sums = jnp.concatenate([total(one) for one in acc], 1)
        mean = sums / n_own

        def centred(start, acc):
            rows = pl.ds(start, SIDE)
            d = cv[z, rows, :] - mean
            return acc + fold(d * d * mask_cols[t, rows, :])

        m2 = total(grid_rows(centred, jnp.zeros((8, C), F32)))
        msg[z, 0:1, 0:C] = sums
        msg[z, 0:1, C:CP] = jnp.broadcast_to(n_own, (1, CP - C))
        msg[z, 1:2, 0:C] = m2
        send_stats(z)

    def peers(body, init):
        if n_dp > 16:
            return lax.fori_loop(0, n_dp - 1, body, init)
        for d in range(n_dp - 1):
            init = body(d, init)
        return init

    def gather_stats(r):
        def add(d, carry):
            return carry + land[r, d]
        return peers(add, msg[r])

    def norm_stats(z):
        sums = gather_stats(z)[0:1, :]
        count = sums[:, CP - 1 : CP]
        mean = sums[:, 0:C] / count

        def spread(values):
            n = values[0:1, CP - 1 : CP]
            off = values[0:1, 0:C] / n - mean
            return values[1:2, 0:C] + n * off * off

        def add(d, carry):
            return carry + spread(land[z, d])
        m2 = peers(add, spread(msg[z]))
        scale = lax.rsqrt(m2 / count + EPS)
        stat[z, 0:1, :] = scale
        stat[z, 1:2, :] = jnp.broadcast_to(count, (1, C))
        return mean, scale

    def mixers(k, backward):
        _, j_g = one_hots(GROUP)
        ww = pack[k, WW : WW + SIDE, 0:SIDE].astype(BF16)
        hw = pack[k, HW : HW + SIDE, 0:SIDE].astype(BF16)
        side_of = 0 if backward else 1
        j_b = jnp.where(j_g, 1.0, 0.0).astype(BF16)
        left = dot(j_b, ww, (1, 1 - side_of)).astype(BF16)
        p = grid_row(lax.broadcasted_iota(jnp.int32, (GROUP, GROUP), 0))
        q = grid_row(lax.broadcasted_iota(jnp.int32, (GROUP, GROUP), 1))
        kw[...] = jnp.where(p == q, dot(left, j_b, (1, 1)), 0.0).astype(BF16)
        spread = dot(hw, i_hot[...], (side_of, 1))
        own = own_column[...]
        for i in range(0, SIDE, 2):
            two = jnp.concatenate([spread[i : i + 1, :] * own, spread[i + 1 : i + 2, :] * own], 0)
            kh[i * SIDE : i * SIDE + 2 * SIDE, :] = two.astype(BF16)
        if not backward:
            i_r, j_r = one_hots(ROWS)
            wb = pack[k, WBIAS : WBIAS + 1, 0:SIDE]
            hb = pack[k, HBIAS : HBIAS + 1, 0:SIDE]
            wbcol[...] = jnp.sum(jnp.where(j_r, wb, 0.0), 1, keepdims=True)
            hbcol[...] = jnp.sum(jnp.where(i_r, hb, 0.0), 1, keepdims=True)

    stored = ((hidden, sp_hidden), (gp, sp_gp), (joined, sp_joined), (normal, sp_normal), (xl, sp_xl))

    def spill(t):
        return [pltpu.make_async_copy(v.at[t], h.at[t], spill_sems.at[t, n]) for n, (v, h) in enumerate(stored)]

    def fetch(t):
        return [pltpu.make_async_copy(h.at[t], v.at[t], fetch_sems.at[t, n]) for n, (v, h) in enumerate(stored)]

    def forward_stage(t, k):
        z = 2 * k + t

        @pl.when(k == 1)
        def _():
            for copy in spill(t):
                copy.wait()

        wait_stats(z)
        mean, scale = norm_stats(z)
        gain = pack[k, BGAIN : BGAIN + 1, :]
        bias = pack[k, BBIAS : BBIAS + 1, :]

        def standardize(start, carry):
            for o in range(0, GROUP, TILE):
                rows = pl.ds(start + o, TILE)
                x = (cv[z, rows, :] - mean) * scale
                cv[z, rows, :] = x
                joined[t, rows, 2 * C : 3 * C] = ((x * gain + bias) * mask_cols[t, rows, :]).astype(BF16)
            along = dot(kw[...], joined[t, pl.ds(start, GROUP), 2 * C : 3 * C])
            for o in range(0, GROUP, TILE):
                rows = pl.ds(start + o, TILE)
                joined[t, rows, 0:C] = (along[o : o + TILE] + wbcol[rows, :]).astype(BF16)
            return carry
        groups(standardize, 0)

        m_bias = pack[k, MBIAS : MBIAS + 1, :]
        n_gain = pack[k, NGAIN : NGAIN + 1, :]
        n_bias = pack[k, NBIAS : NBIAS + 1, :]
        d_bias = pack[k, DBIAS : DBIAS + 1, :]
        u_bias = [pack[k, UBIAS + n : UBIAS + n + 1, 0:FT] for n in range(FF // FT)]

        def rest(start, carry):
            rows = pl.ds(start, GROUP)
            along = dot(kh[rows, :], joined[t, :, 2 * C : 3 * C])
            for o in range(0, GROUP, TILE):
                part = pl.ds(start + o, TILE)
                joined[t, part, C : 2 * C] = (along[o : o + TILE] + hbcol[part, :]).astype(BF16)
            merged = dot(joined[t, rows, :], wm[k], (1, 1))
            for o in range(0, GROUP, TILE):
                part = pl.ds(start + o, TILE)
                f = uf[t, pl.ds(start + SIDE + o, TILE), :] + merged[o : o + TILE] + m_bias
                d = f - jnp.mean(f, 1, keepdims=True)
                rs = lax.rsqrt(jnp.mean(d * d, 1, keepdims=True) + EPS)
                x = d * rs
                first[part, :] = f
                rstd[z, part, :] = rs
                xl[t, part, :] = x.astype(BF16)
                normal[t, part, :] = (x * n_gain + n_bias).astype(BF16)
            norm = normal[t, rows, :]
            pre = dot(norm, wu[k, :, 0:FT])
            for n in range(FF // FT):
                cols = slice(n * FT, n * FT + FT)
                now = pre
                if n + 1 < FF // FT:
                    pre = dot(norm, wu[k, :, n * FT + FT : n * FT + 2 * FT])
                for o in range(0, GROUP, TILE):
                    part = pl.ds(start + o, TILE)
                    h, dh = gelu_both(now[o : o + TILE] + u_bias[n])
                    hidden[t, part, cols] = h.astype(BF16)
                    gp[t, part, cols] = dh.astype(BF16)
            down = dot(hidden[t, rows, :], wd[k], (1, 1))
            i = start // SIDE
            for r in range(GROUP // SIDE):
                y = first[pl.ds(start + r * SIDE, SIDE), :] + down[r * SIDE : r * SIDE + SIDE] + d_bias
                ybuf[z, i + r] = y.astype(BF16)
            return carry
        groups(rest, 0)

        @pl.when(k == 0)
        def _():
            def reread(start, carry):
                uf[t, pl.ds(start + SIDE, SIDE), :] = ybuf[z, lax.div(start, SIDE)].astype(F32)
                return carry
            grid_rows(reread, 0)

        @pl.when(me_p == k)
        def _():
            pltpu.make_async_copy(ybuf.at[z], so_h.at[0, 2 * me_p + t], so_local.at[t]).start()

        @pl.when(me_p != k)
        def _():
            across(ybuf.at[z], so_h.at[0, 2 * me_p + t], so_send.at[t], so_recv.at[t]).start()

    def backward_stage(t, k, tick):
        z = 2 * k + t
        zero = jnp.zeros((8, C), F32)
        n_gain = pack[k, NGAIN : NGAIN + 1, :]

        d_acc = zero
        for o in range(0, ROWS, TILE):
            g = gf[t, o : o + TILE, :]
            gb[o : o + TILE, :] = g.astype(BF16)
            d_acc = d_acc + fold(g)
        gs[k, DBIAS : DBIAS + 1, :] += total(d_acc)
        gbt[...] = gb[...].T
        for n in range(2):
            acc_d[k, n] += dot(gbt[...], hidden[t, :, n * WIDE : n * WIDE + WIDE])
        tick(1)

        def chain(start, acc):
            rows = pl.ds(start, GROUP)
            x_acc, n_acc, m_acc, u_acc = acc
            u_acc = list(u_acc)
            low = gb[rows, :]
            raw = dot(low, wd[k, :, 0:FT])
            for n in range(FF // FT):
                cols = slice(n * FT, n * FT + FT)
                now = raw
                if n + 1 < FF // FT:
                    raw = dot(low, wd[k, :, n * FT + FT : n * FT + 2 * FT])
                for o in range(0, GROUP, TILE):
                    part = pl.ds(start + o, TILE)
                    gpn = (now[o : o + TILE] * gp[t, part, cols].astype(F32)).astype(BF16)
                    gpre[part, cols] = gpn
                    u_acc[n] = u_acc[n] + fold(gpn.astype(F32))
            back = dot(gpre[rows, :], wu[k], (1, 1))
            for o in range(0, GROUP, TILE):
                part = pl.ds(start + o, TILE)
                g = back[o : o + TILE]
                x = xl[t, part, :].astype(F32)
                gn = g * n_gain
                mean_g = jnp.mean(gn, 1, keepdims=True)
                mean_gx = jnp.mean(gn * x, 1, keepdims=True)
                out = gf[t, part, :] + rstd[z, part, :] * (gn - mean_g - x * mean_gx)
                gf[t, part, :] = out
                low = out.astype(BF16)
                gmb[part, :] = low
                x_acc = x_acc + fold(g * x)
                n_acc = n_acc + fold(g)
                m_acc = m_acc + fold(low.astype(F32))
            low = gmb[rows, :]
            g_w = dot(low, wm[k, :, 0:C])
            g_h = dot(low, wmid[k])
            for o in range(0, GROUP, TILE):
                part = pl.ds(start + o, TILE)
                one = g_w[o : o + TILE].astype(BF16)
                gwb[o : o + TILE, :] = one
                wcol[part, :] += jnp.sum(one.astype(F32), 1, keepdims=True)
                one = g_h[o : o + TILE].astype(BF16)
                gwh[part, :] = one
                hcol[part, :] += jnp.sum(one.astype(F32), 1, keepdims=True)
            third = dot(low, wm[k, :, 2 * C : 3 * C])
            crossed = dot(kw[...], gwb[...])
            for o in range(0, GROUP, TILE):
                gmix[t, pl.ds(start + o, TILE), :] = third[o : o + TILE] + crossed[o : o + TILE]
            gw_acc[...] += dot(gwb[...], joined[t, rows, 2 * C : 3 * C], (1, 1))
            return (x_acc, n_acc, m_acc, u_acc)
        acc = groups(chain, (zero, zero, zero, [jnp.zeros((8, FT), F32) for _ in range(FF // FT)]))
        tick(4)
        gs[k, NGAIN : NGAIN + 1, :] += total(acc[0])
        gs[k, NBIAS : NBIAS + 1, :] += total(acc[1])
        gs[k, MBIAS : MBIAS + 1, :] += total(acc[2])
        for n in range(FF // FT):
            gs[k, UBIAS + n : UBIAS + n + 1, 0:FT] += total(acc[3][n])
        gbt[...] = normal[t].T
        for n in range(2):
            acc_u[k, n] += dot(gbt[...], gpre[:, n * WIDE : n * WIDE + WIDE])
        tick(5)
        gbt[...] = gmb[...].T
        for n in range(2):
            width = min(MT, 3 * C - n * MT)
            acc_m[k, n, :, 0:width] += dot(gbt[...], joined[t, :, n * MT : n * MT + width])
        tick(6)
        gh_acc[...] += dot(gwh[...], joined[t, :, 2 * C : 3 * C], (1, 1))
        tick(10)

        def batch_sums(start, acc):
            plain, cross = acc
            crossed = dot(kh[pl.ds(start, GROUP), :], gwh[...])
            for o in range(0, GROUP, TILE):
                rows = pl.ds(start + o, TILE)
                g = (gmix[t, rows, :] + crossed[o : o + TILE]) * mask_cols[t, rows, :]
                gmix[t, rows, :] = g
                plain = plain + fold(g)
                cross = cross + fold(g * cv[z, rows, :])
            return plain, cross
        acc = groups(batch_sums, (zero, zero))
        plain, cross = total(acc[0]), total(acc[1])
        gs[k, BBIAS : BBIAS + 1, :] += plain
        gs[k, BGAIN : BGAIN + 1, :] += cross
        r = 4 + z
        msg[r, 0:1, 0:C] = plain
        msg[r, 1:2, 0:C] = cross
        send_stats(r)

    def input_stage(t, k, tick):
        z = 2 * k + t
        r = 4 + z
        wait_stats(r)
        scale, count = stat[z, 0:1, :], stat[z, 1:2, :]
        both = gather_stats(r)
        plain, cross = both[0:1, 0:C], both[1:2, 0:C]
        gain = pack[k, BGAIN : BGAIN + 1, :]
        out_scale = gain * scale
        plain = plain / count
        cross = cross / count

        def shifted(start, carry):
            rows = pl.ds(start, SIDE)
            g = (gmix[t, rows, :] - plain - cv[z, rows, :] * cross) * (mask_cols[t, rows, :] * out_scale)
            rows = pl.ds(start + SIDE, SIDE)
            gsh[0, rows, :] = sooner(g)
            gsh[1, rows, :] = g
            gsh[2, rows, :] = later(g)
            return carry
        grid_rows(shifted, 0)
        tick(8)
        taps = [[pack[k, CONV + n : CONV + n + 1, l:m] for n in range(9)] for l, m in LANES]

        def pull(start, acc):
            new = []
            for (l, m), tap, one in zip(LANES, taps, acc):
                u = [uf[t, pl.ds(start + SIDE * r, SIDE), l:m] for r in range(3)]
                out = gf[t, pl.ds(start, SIDE), l:m]
                sums = []
                for s in range(3):
                    around = [gsh[s, pl.ds(start + SIDE * r, SIDE), l:m] for r in range(3)]
                    out = out + around[2] * tap[s] + around[1] * tap[3 + s] + around[0] * tap[6 + s]
                    sums.append([one[s][r] + fold(around[1] * u[r]) for r in range(3)])
                new.append(sums)
                igbuf[z, lax.div(start, SIDE), :, l:m] = out.astype(BF16)
            return new
        acc = grid_rows(pull, [[[jnp.zeros((8, m - l), F32) for _ in range(3)] for _ in range(3)] for l, m in LANES])
        for (l, m), one in zip(LANES, acc):
            for r in range(3):
                for s in range(3):
                    row = CONV + 3 * r + s
                    gs[k, row : row + 1, l:m] += total(one[s][r])

        @pl.when(k == 1)
        def _():
            def reread(start, carry):
                gf[t, pl.ds(start, SIDE), :] = igbuf[z, lax.div(start, SIDE)].astype(F32)
                return carry
            grid_rows(reread, 0)

        @pl.when(me_p == k)
        def _():
            pltpu.make_async_copy(igbuf.at[z], ig_h.at[0, 2 * me_p + t], ig_local.at[t]).start()

        @pl.when(me_p != k)
        def _():
            across(igbuf.at[z], ig_h.at[0, 2 * me_p + t], ig_send.at[t], ig_recv.at[t]).start()

    def clear_mix():
        gw_acc[...] = jnp.zeros(gw_acc.shape, F32)
        gh_acc[...] = jnp.zeros(gh_acc.shape, F32)
        wcol[...] = jnp.zeros(wcol.shape, F32)
        hcol[...] = jnp.zeros(hcol.shape, F32)

    def close_mix(k):
        i_r, j_r = one_hots(ROWS)
        _, j_g = one_hots(GROUP)
        gs[k, WBIAS : WBIAS + 1, 0:SIDE] = total(jnp.where(j_r, wcol[...], 0.0))
        gs[k, HBIAS : HBIAS + 1, 0:SIDE] = total(jnp.where(i_r, hcol[...], 0.0))
        highest = lax.Precision.HIGHEST
        p = grid_row(lax.broadcasted_iota(jnp.int32, (GROUP, GROUP), 0))
        q = grid_row(lax.broadcasted_iota(jnp.int32, (GROUP, GROUP), 1))
        own = jnp.where(p == q, gw_acc[...], 0.0)
        own = jnp.sum(own.reshape(GROUP // SIDE, SIDE, GROUP), 0)
        gs[k, WW : WW + SIDE, 0:SIDE] = dot(own, jnp.where(j_g, 1.0, 0.0), precision=highest)
        i_f = jnp.where(i_r, 1.0, 0.0)
        for i in range(SIDE):
            rows = slice(i * SIDE, i * SIDE + SIDE)
            own = total(fold(own_column[...] * gh_acc[rows, :]))
            first[i : i + 1, :] = own[:, 0:C]
            gnorm[i : i + 1, 0 : ROWS - C] = own[:, C:ROWS]
        value = dot(first[0:SIDE, :], i_f[0:C, :], precision=highest)
        value += dot(gnorm[0:SIDE, 0 : ROWS - C], i_f[C:ROWS, :], precision=highest)
        gs[k, HW : HW + SIDE, 0:SIDE] = value

    bits = [1, 2]
    while 2 * bits[-1] < n_dp:
        bits.append(2 * bits[-1])
    n_swaps = len(bits) - 2
    n_steps = 1 + 2 + n_swaps + 2

    def partner(bit):
        return me_d + bit * (1 - 2 * lax.rem(me_d // bit, 2))

    def side(bit):
        return lax.rem(me_d // bit, 2)

    def along(bit, src, dst, send, recv):
        return pltpu.make_async_remote_copy(
            src_ref=src, dst_ref=dst, send_sem=send, recv_sem=recv,
            device_id={"dp": partner(bit)}, device_id_type=MESH)

    streams = (
        (acc_d, gd_h, sb_d, lb_d, rl_d), (acc_u, gu_h, sb_u, lb_u, rl_u), (acc_m, gm_h, sb_m, lb_m, rl_m))

    def reduction(k, which):
        acc, out_h, sb, lb, rl = streams[which]
        sb, lb, rl = sb.at[k], lb.at[k], rl.at[k]
        halving = [1 + me_p, 2 - me_p] if which != 1 else [2 - me_p, 1 + me_p]

        def sems(step):
            return red_send.at[3 * k + which, step], red_recv.at[3 * k + which, step]

        def own(q):
            return k, lax.div(q, 2), pl.ds(pl.multiple_of(me_p * HALF + lax.rem(q, 2) * SHARD, 16), SHARD), slice(None)

        def each(count, body):
            if count == 1:
                body(0)
                return

            def step(n, carry):
                body(n)
                return carry
            lax.fori_loop(0, count, step, 0)

        in_chip = across(sb.at[pl.ds(0, SHARDS)], lb, *sems(0))
        base = [0]
        for n, bit in enumerate(halving):
            base.append(base[n] + side(bit) * (2 >> n))
        mine = base[2]

        def half_copy(n):
            count, at = 2 >> n, 2 * n
            return along(halving[n], sb.at[pl.ds(at, count)], rl.at[pl.ds(at, count)], *sems(1 + n))

        def swap_copy(n):
            return along(bits[2 + n], sb.at[3 + n], rl.at[3 + n], *sems(3 + n))

        def double_copy(n):
            count = 2 >> n
            here = lb.at[pl.ds(base[n + 1], count)]
            return along(halving[n], here, here, *sems(n_steps - 1 - n))

        def send_half(n, landed):
            count, at = 2 >> n, 2 * n
            give = base[n] + (1 - side(halving[n])) * count
            keep = base[n + 1]

            def one(q):
                sb[at + q] = (acc[own(give + q)] + landed(give + q).astype(F32)).astype(BF16)
            each(count, one)
            half_copy(n).start()

            def two(q):
                acc[own(keep + q)] += landed(keep + q).astype(F32)
            each(count, two)

        def start():
            def one(q):
                rows = pl.ds(pl.multiple_of(other * HALF + lax.rem(q, 2) * SHARD, 16), SHARD)
                sb[q] = acc[k, lax.div(q, 2), rows, :].astype(BF16)
            each(SHARDS, one)
            in_chip.start()

        def first_half():
            in_chip.wait()
            send_half(0, lambda q: lb[q])

        def second_half():
            half_copy(0).wait()
            send_half(1, lambda q: rl[q - base[1]])

        def swap(n):
            def run():
                if n == 0:
                    half_copy(1).wait()
                    sb[3] = (acc[own(mine)] + rl[2].astype(F32)).astype(BF16)
                else:
                    swap_copy(n - 1).wait()
                    sb[3 + n] = (sb[2 + n].astype(F32) + rl[2 + n].astype(F32)).astype(BF16)
                swap_copy(n).start()
            return run

        def double(n):
            def run():
                if n == 1:
                    last = n_swaps - 1
                    swap_copy(last).wait()
                    lb[mine] = (sb[3 + last].astype(F32) + rl[3 + last].astype(F32)).astype(BF16)
                else:
                    double_copy(n + 1).wait()
                double_copy(n).start()
            return run

        def hand_over():
            double_copy(0).wait()

            @pl.when(me_p == k)
            def _():
                pltpu.make_async_copy(lb, out_h.at[me_p], out_local.at[which]).start()

            @pl.when(me_p != k)
            def _():
                across(lb, out_h.at[me_p], out_send.at[which], out_recv.at[which]).start()

        return [start, first_half, second_half] + [swap(n) for n in range(n_swaps)] + [double(1), double(0), hand_over]

    def small_sum(rows, landing, send, recv):
        count = rows.stop - rows.start
        rows = pl.ds(rows.start, count)
        in_chip = across(gs.at[other, rows], landing.at[0], send.at[0], recv.at[0])

        def swap_copy(n):
            return along(bits[n], gs.at[me_p, rows], landing.at[1 + n], send.at[1 + n], recv.at[1 + n])

        def step(n):
            def run():
                (swap_copy(n - 1) if n else in_chip).wait()
                gs[me_p, rows, :] += landing[n]
                if n < len(bits):
                    swap_copy(n).start()
            return run
        return [in_chip.start] + [step(n) for n in range(len(bits) + 1)]

    small = small_sum(slice(SMALL, PACK), small_land, small_send, small_recv)
    taps_sum = small_sum(slice(0, SMALL), conv_land, conv_send, conv_recv)

    plan = {}
    backward_places, input_places = [0, 1, 4, 5, 6, 10, 11], [7, 8, 9]
    order = []
    for n in range(6):
        order += [(n, p) for p in input_places] if n > 1 else []
        order += [(n, p) for p in backward_places] if n < 4 else []

    def put(start, steps, gap):
        at = order.index(start)
        steps = list(steps)
        while steps and at < len(order):
            plan.setdefault(order[at], []).append(steps.pop(0))
            at += gap
        return steps

    for which, place in enumerate((1, 5, 6)):
        assert not put((1, place), reduction(1, which), 2 if n_swaps < 3 else 1)
    tails = [put((3, place), reduction(0, which), 1) for which, place in enumerate((1, 5, 6))]
    tails.append(put((4, 7), small, 1))
    tails.append(list(taps_sum))

    pack_over.wait()
    for t in range(2):
        image_in[t].wait()

    def widen_image(t):
        def widen(i, inner):
            uf[t, pl.ds(pl.multiple_of(i * SIDE + SIDE, SIDE), SIDE), :] = ub[t, i].astype(F32)
            return inner
        lax.fori_loop(0, SIDE, widen, 0)

    def start_image(t, carry):
        widen_image(t)
        conv_stage(t, 0)
        return carry
    lax.fori_loop(0, 2, start_image, 0)
    for t in range(2):
        grad_in[t].start()

    for copy in weights_in + weights_over:
        copy.wait()
    for k in range(2):
        wmid[k] = wm[k, :, C : 2 * C]

    def forward_block(k, carry):
        mixers(k, False)

        def one(t, inner):
            forward_stage(t, k)

            @pl.when(k == 0)
            def _():
                for copy in spill(t):
                    copy.start()
                conv_stage(t, 1)
            return inner
        lax.fori_loop(0, 2, one, 0)
        return carry
    lax.fori_loop(0, 2, forward_block, 0)

    for t in range(2):
        grad_in[t].wait()
        pltpu.make_async_copy(ybuf.at[t], so_h.at[0, t], so_local.at[t]).wait()
        across(ybuf.at[t], so_h.at[0, t], so_send.at[t], so_recv.at[t]).wait_send()

    def load_grad(t, carry):
        def widen(i, inner):
            gf[t, pl.ds(pl.multiple_of(i * SIDE, SIDE), SIDE), :] = ub[t, i].astype(F32)
            return inner
        lax.fori_loop(0, SIDE, widen, 0)
        return carry
    lax.fori_loop(0, 2, load_grad, 0)
    for t in range(2):
        image_copy(t, again_sems.at[t]).start()

    def turn(s, carry):
        t = lax.rem(s, 2)

        def tick(place):
            for n in range(6):
                steps = plan.get((n, place), [])
                if steps:
                    @pl.when(s == n)
                    def _():
                        for step in steps:
                            step()

        @pl.when(lax.rem(s, 2) == 0)
        def _():
            @pl.when(s > 0)
            def _():
                close_mix(2 - lax.div(s, 2))

            @pl.when(s < 4)
            def _():
                mixers(1 - lax.div(s, 2), True)
                clear_mix()

        @pl.when(s > 1)
        def _():
            @pl.when(s > 3)
            def _():
                image_copy(t, again_sems.at[t]).wait()
                widen_image(t)
            tick(7)
            input_stage(t, 2 - lax.div(s, 2), tick)
            tick(9)

        @pl.when(s < 4)
        def _():
            @pl.when(s > 1)
            def _():
                for copy in fetch(t):
                    copy.wait()
            tick(0)
            backward_stage(t, 1 - lax.div(s, 2), tick)
            tick(11)

            @pl.when(s < 2)
            def _():
                for copy in fetch(t):
                    copy.start()
        return carry
    lax.fori_loop(0, 6, turn, 0)

    while any(tails):
        for steps in tails:
            if steps:
                steps.pop(0)()

    gs_out = pltpu.make_async_copy(gs.at[me_p], gs_h, gs_sem.at[0])
    gs_out.start()
    for t in range(2):
        pltpu.make_async_copy(igbuf.at[t], ig_h.at[0, t], ig_local.at[t]).wait()
        across(ybuf.at[t], so_h.at[0, t], so_send.at[t], so_recv.at[t]).wait_recv()
        across(igbuf.at[t], ig_h.at[0, t], ig_send.at[t], ig_recv.at[t]).wait()
    for n, (_, out_h, _, lb, _) in enumerate(streams):
        pltpu.make_async_copy(lb.at[0], out_h.at[0], out_local.at[n]).wait()
        across(lb.at[0], out_h.at[0], out_send.at[n], out_recv.at[n]).wait()
    gs_out.wait()


def finish_kernel(
    so_in, ig_in, gd_in, gu_in, gm_in, gs,
    so, ig, conv, bgain, bbias, ww, wb, hw, hb, gm, mbias, ngain, nbias, gu, ubias, gd, dbias,
    large, d_in, u_in, m_in, d_out, u_out, m_out, in_sems, out_sems,
):
    moved = ((gd_in, d_in), (gu_in, u_in), (gm_in, m_in), (so_in, large.at[0]), (ig_in, large.at[1]))
    arrive = [pltpu.make_async_copy(src, dst, in_sems.at[n]) for n, (src, dst) in enumerate(moved)]
    for copy in arrive:
        copy.start()
    moved = ((d_out, gd), (u_out, gu), (m_out, gm), (large.at[0], so), (large.at[1], ig))
    leave = [pltpu.make_async_copy(src, dst, out_sems.at[n]) for n, (src, dst) in enumerate(moved)]
    for n in range(9):
        conv[n] = gs[CONV + n : CONV + n + 1, :]
    for row, ref in ((BGAIN, bgain), (BBIAS, bbias), (MBIAS, mbias), (NGAIN, ngain), (NBIAS, nbias), (DBIAS, dbias)):
        ref[...] = gs[row : row + 1, :]
    for row, ref in ((WBIAS, wb), (HBIAS, hb)):
        ref[...] = gs[row : row + 1, 0:SIDE]
    for n in range(FF // FT):
        ubias[:, n * FT : n * FT + FT] = gs[UBIAS + n : UBIAS + n + 1, 0:FT]
    for row, ref in ((WW, ww), (HW, hw)):
        ref[0] = gs[row : row + SIDE, 0:SIDE]
    for n, (src, dst, piece) in enumerate(((d_in, d_out, WIDE), (u_in, u_out, WIDE), (m_in, m_out, MT))):
        arrive[n].wait()
        for p in range(2):
            for q in range(SHARDS):
                start, at = p * HALF + (q % 2) * SHARD, piece * (q // 2)
                width = min(piece, dst.shape[1] - at)
                dst[start : start + SHARD, at : at + width] = src[p, q, :, 0:width].astype(F32)
        leave[n].start()
    for n in (3, 4):
        arrive[n].wait()
        leave[n].start()
    for copy in leave:
        copy.wait()


def on_device(
    images, masks, conv_weight, batch_gain, batch_bias, width_weight, width_bias,
    height_weight, height_bias, merge_weight, merge_bias, norm_gain, norm_bias,
    up_weight, up_bias, down_weight, down_bias, out_grad,
):
    n_dp = lax.axis_size("dp")
    micro = images.shape[0]
    steps = max(n_dp.bit_length() - 1, 4)
    any_space = pl.BlockSpec(memory_space=pl.ANY)
    vmem = pl.BlockSpec(memory_space=pltpu.VMEM)
    dma = pltpu.SemaphoreType.DMA
    grid = (SIDE, SIDE, C)
    shape = jax.ShapeDtypeStruct
    outs = pl.pallas_call(
        functools.partial(kernel, n_dp),
        out_shape=(
            shape((1, micro) + grid, BF16),
            shape((1, micro) + grid, BF16),
            shape((2, SHARDS, SHARD, WIDE), BF16),
            shape((2, SHARDS, SHARD, WIDE), BF16),
            shape((2, SHARDS, SHARD, MT), BF16),
            shape((PACK, C), F32),
            shape((2, ROWS, FF), BF16),
            shape((2, ROWS, FF), BF16),
            shape((2, ROWS, 3 * C), BF16),
            shape((2, ROWS, C), BF16),
            shape((2, ROWS, C), BF16),
        ),
        in_specs=[any_space] + [vmem] * 8 + [any_space] + [vmem] * 3 + [any_space, vmem, any_space, vmem, any_space],
        out_specs=(any_space,) * 11,
        scratch_shapes=[
            pltpu.VMEM((2, ROWS, 1), F32),
            pltpu.VMEM((4, 2, C), F32),
            pltpu.VMEM((SIDE, ROWS), F32),
            pltpu.VMEM((ROWS, SIDE), BF16),
            pltpu.VMEM((2, PACK, C), F32),
            pltpu.VMEM((2, C, 3 * C), BF16),
            pltpu.VMEM((2, C, C), BF16),
            pltpu.VMEM((2, C, FF), BF16),
            pltpu.VMEM((2, C, FF), BF16),
            pltpu.VMEM((2,) + grid, BF16),
            pltpu.VMEM((2, ROWS + 2 * SIDE, C), F32),
            pltpu.VMEM((4, ROWS, C), F32),
            pltpu.VMEM((2, ROWS, 3 * C), BF16),
            pltpu.VMEM((2, ROWS, C), BF16),
            pltpu.VMEM((2, ROWS, C), BF16),
            pltpu.VMEM((4, ROWS, 1), F32),
            pltpu.VMEM((2, ROWS, FF), BF16),
            pltpu.VMEM((2, ROWS, FF), BF16),
            pltpu.VMEM((2, ROWS, C), F32),
            pltpu.VMEM((ROWS, C), BF16),
            pltpu.VMEM((ROWS, C), BF16),
            pltpu.VMEM((GROUP, C), BF16),
            pltpu.VMEM((C, ROWS), BF16),
            pltpu.VMEM((ROWS, FF), BF16),
            pltpu.VMEM((2, ROWS, C), F32),
            pltpu.VMEM((ROWS, C), BF16),
            pltpu.VMEM((3, ROWS + 2 * SIDE, C), F32),
            pltpu.VMEM((GROUP, GROUP), BF16),
            pltpu.VMEM((ROWS, ROWS), BF16),
            pltpu.VMEM((ROWS, 1), F32),
            pltpu.VMEM((ROWS, 1), F32),
            pltpu.VMEM((GROUP, GROUP), F32),
            pltpu.VMEM((ROWS, ROWS), F32),
            pltpu.VMEM((ROWS, 1), F32),
            pltpu.VMEM((ROWS, 1), F32),
            pltpu.VMEM((4,) + grid, BF16),
            pltpu.VMEM((8, 2, CP), F32),
            pltpu.VMEM((8, n_dp - 1, 2, CP), F32),
            pltpu.VMEM((2, 2, C, WIDE), F32),
            pltpu.VMEM((2, 2, C, WIDE), F32),
            pltpu.VMEM((2, 2, C, MT), F32),
            pltpu.VMEM((2, PACK, C), F32),
            pltpu.VMEM((2, 1 + steps, SHARD, WIDE), BF16),
            pltpu.VMEM((2, SHARDS, SHARD, WIDE), BF16),
            pltpu.VMEM((2, 1 + steps, SHARD, WIDE), BF16),
            pltpu.VMEM((2, 1 + steps, SHARD, WIDE), BF16),
            pltpu.VMEM((2, SHARDS, SHARD, WIDE), BF16),
            pltpu.VMEM((2, 1 + steps, SHARD, WIDE), BF16),
            pltpu.VMEM((2, 1 + steps, SHARD, MT), BF16),
            pltpu.VMEM((2, SHARDS, SHARD, MT), BF16),
            pltpu.VMEM((2, 1 + steps, SHARD, MT), BF16),
            pltpu.VMEM((1 + steps, PACK - SMALL, C), F32),
            pltpu.VMEM((1 + steps, SMALL, C), F32),
            dma((9,)), dma((2,)), dma((2,)), dma((3,)), dma((3,)), dma((8,)), dma((8,)),
            dma((2,)), dma((2,)), dma((2,)), dma((2,)), dma((2,)), dma((2,)), dma((2, 5)), dma((2, 5)),
            dma((6, 3 + steps)), dma((6, 3 + steps)), dma((1 + steps,)), dma((1 + steps,)),
            dma((1 + steps,)), dma((1 + steps,)), dma((3,)), dma((3,)), dma((3,)), dma((1,)),
        ],
        compiler_params=pltpu.CompilerParams(
            collective_id=0, has_side_effects=True, vmem_limit_bytes=65400 * 1024),
    )(
        images, masks, conv_weight, batch_gain, batch_bias, width_weight, width_bias, height_weight, height_bias,
        merge_weight[0].T, merge_bias, norm_gain, norm_bias, up_weight[0], up_bias, down_weight[0].T, down_bias, out_grad)

    row = shape((1, C), F32)
    square, line = shape((1, SIDE, SIDE), F32), shape((1, SIDE), F32)
    so, ig, conv, bgain, bbias, ww, wb, hw, hb, gm, mbias, ngain, nbias, gu, ubias, gd, dbias = pl.pallas_call(
        finish_kernel,
        out_shape=(
            shape((1, micro) + grid, BF16), shape((1, micro) + grid, BF16), shape((9, 1, C), F32), row, row,
            square, line, square, line, shape((C, 3 * C), F32), row, row, row,
            shape((C, FF), F32), shape((1, FF), F32), shape((C, FF), F32), row),
        in_specs=[any_space] * 5 + [vmem],
        out_specs=(any_space,) * 2 + (vmem,) * 7 + (any_space,) + (vmem,) * 3 + (any_space, vmem, any_space, vmem),
        scratch_shapes=[
            pltpu.VMEM((2, 1, micro) + grid, BF16),
            pltpu.VMEM((2, SHARDS, SHARD, WIDE), BF16),
            pltpu.VMEM((2, SHARDS, SHARD, WIDE), BF16),
            pltpu.VMEM((2, SHARDS, SHARD, MT), BF16),
            pltpu.VMEM((C, FF), F32),
            pltpu.VMEM((C, FF), F32),
            pltpu.VMEM((C, 3 * C), F32),
            dma((5,)), dma((5,)),
        ],
        compiler_params=pltpu.CompilerParams(vmem_limit_bytes=65400 * 1024),
    )(*outs[:6])
    return (
        so, ig, jnp.swapaxes(conv, 0, 1), bgain, bbias, ww, wb, hw, hb, gm.T[None], mbias, ngain, nbias,
        gu[None], ubias, gd.T[None], dbias)


def solution(mesh):
    data4 = P("dp", None, None, None)
    p1, p2, p3 = P("pipe"), P("pipe", None), P("pipe", None, None)
    out5 = P("pipe", "dp", None, None, None)
    return jax.shard_map(
        on_device,
        mesh=mesh,
        in_specs=(data4, P("dp", None, None), p3, p2, p2, p3, p2, p3, p2, p3, p2, p2, p2, p3, p2, p3, p2, data4),
        out_specs=(out5, out5, p3, p2, p2, p3, p2, p3, p2, p3, p2, p2, p2, p3, p2, p3, p2),
        check_vma=False,
    )
```

profile of v0, /device:TPU:0, one launch (start us, length us, event | category | flops | bytes accessed | tf_op | source)
XLA Modules:
  0.0 180.0 jit_solution(1162835991807726875)
XLA Ops:
  0.7 172.4 %shard_map.305 = (bf16[1,4,24,24,320]{4,3,2,1,0:T(8,128)(2,1)}, bf16[1,4,24,24,320]{4,3,2,1,0:T(8,128)(2,1)}, bf16[2,4,80,640]{3,2,1,0:T(8,128)(2,1)}, bf16[2,4,...) custom-call(bf16[4,24,24,320]{3,2,1,0:T(8,128)(2,1)} %images.1, ...), custom_call_target="tpu_custom_call" | custom-call | tf_op jit(solution)/shard_map/pallas_call | solution.py:891
  173.1 6.7 %shard_map.306 = (bf16[1,4,24,24,320]{4,3,2,1,0:T(8,128)(2,1)}, bf16[1,4,24,24,320]{4,3,2,1,0:T(8,128)(2,1)}, f32[9,1,320]{2,1,0:T(1,128)}, f32[1,320]{1,0:T(1,1...) custom-call(bf16[1,4,24,24,320]{4,3,2,1,0:T(8,128)(2,1)} %get-tuple-, ...), custom_call_target="tpu_custom_call" | custom-call | tf_op jit(solution)/shard_map/pallas_call | solution.py:975
where the time goes:
time: 180 us
  Pallas kernels  179 us (99%)
    pallas_call x1, Pallas kernels, on_device(): pl.pallas_call(functools.partial(kernel, n_dp), out_shape=(shape((1, micr...  172 us
    pallas_call x1, Pallas kernels, on_device(): pl.pallas_call(finish_kernel, out_shape=(shape((1, micro) + grid, BF16),...  6.75 us

commit v1 on v0

--- a/solution.py
+++ b/solution.py
@@ -28,7 +28,7 @@
 WIDE = FF // 2
 SHARDS = 4
 MT = 512
-STEP = 8
+STEP = 24
 
 CONV, BGAIN, BBIAS, MBIAS, NGAIN, NBIAS, DBIAS, WBIAS, HBIAS, UBIAS, WW, HW, PACK = (
     0, 16, 17, 18, 19, 20, 21, 22, 23, 24, 32, 56, 80)
@@ -39,6 +39,13 @@
     return lax.dot_general(
         a, b, (((contract[0],), (contract[1],)), ((), ())),
         preferred_element_type=F32, precision=precision)
+
+
+def in_turn(phases, starts):
+    for step in range(len(phases) + len(starts) - 1):
+        for g, start in enumerate(starts):
+            if 0 <= step - g < len(phases):
+                phases[step - g](start)
 
 
 def fold(value):
@@ -77,7 +84,7 @@
     images, masks, conv_w, bgain, bbias, wwt, wb, hwt, hb, wm_h, mbias, ngain, nbias, wu_h, ubias, wd_h, dbias, og_h,
     so_h, ig_h, gd_h, gu_h, gm_h, gs_h, sp_hidden, sp_gp, sp_joined, sp_normal, sp_xl,
     mask_cols, stat, own_column, i_hot, pack, wm, wmid, wu, wd, ub, uf, cv, joined, normal, xl, rstd, hidden, gp,
-    gf, gb, gmb, gwb, gbt, gpre, gmix, gwh, gsh, kw, kh, wbcol, hbcol,
+    gf, gb, gmb, gwb, gbt, gmt, gpre, gmix, gwh, gsh, kw, kh, wbcol, hbcol,
     gw_acc, gh_acc, wcol, hcol, ybuf, msg, land, acc_d, acc_u, acc_m, gs,
     sb_d, lb_d, rl_d, sb_u, lb_u, rl_u, sb_m, lb_m, rl_m, small_land, conv_land,
     local_sems, again_sems, pack_sems, w_send, w_recv, st_send, st_recv,
@@ -314,16 +321,21 @@
         d_bias = pack[k, DBIAS : DBIAS + 1, :]
         u_bias = [pack[k, UBIAS + n : UBIAS + n + 1, 0:FT] for n in range(FF // FT)]
 
-        def rest(start, carry):
-            rows = pl.ds(start, GROUP)
+        starts = [g * GROUP for g in range(ROWS // GROUP)]
+        merged, down = {}, {}
+
+        def mix(start):
+            rows = slice(start, start + GROUP)
             along = dot(kh[rows, :], joined[t, :, 2 * C : 3 * C])
             for o in range(0, GROUP, TILE):
-                part = pl.ds(start + o, TILE)
+                part = slice(start + o, start + o + TILE)
                 joined[t, part, C : 2 * C] = (along[o : o + TILE] + hbcol[part, :]).astype(BF16)
-            merged = dot(joined[t, rows, :], wm[k], (1, 1))
+            merged[start] = dot(joined[t, rows, :], wm[k], (1, 1))
+
+        def layer_norm(start):
             for o in range(0, GROUP, TILE):
-                part = pl.ds(start + o, TILE)
-                f = uf[t, pl.ds(start + SIDE + o, TILE), :] + merged[o : o + TILE] + m_bias
+                part = slice(start + o, start + o + TILE)
+                f = uf[t, start + SIDE + o : start + SIDE + o + TILE, :] + merged[start][o : o + TILE] + m_bias
                 d = f - jnp.mean(f, 1, keepdims=True)
                 rs = lax.rsqrt(jnp.mean(d * d, 1, keepdims=True) + EPS)
                 x = d * rs
@@ -331,6 +343,9 @@
                 rstd[z, part, :] = rs
                 xl[t, part, :] = x.astype(BF16)
                 normal[t, part, :] = (x * n_gain + n_bias).astype(BF16)
+
+        def activate(start):
+            rows = slice(start, start + GROUP)
             norm = normal[t, rows, :]
             pre = dot(norm, wu[k, :, 0:FT])
             for n in range(FF // FT):
@@ -339,17 +354,21 @@
                 if n + 1 < FF // FT:
                     pre = dot(norm, wu[k, :, n * FT + FT : n * FT + 2 * FT])
                 for o in range(0, GROUP, TILE):
-                    part = pl.ds(start + o, TILE)
+                    part = slice(start + o, start + o + TILE)
                     h, dh = gelu_both(now[o : o + TILE] + u_bias[n])
                     hidden[t, part, cols] = h.astype(BF16)
                     gp[t, part, cols] = dh.astype(BF16)
-            down = dot(hidden[t, rows, :], wd[k], (1, 1))
-            i = start // SIDE
+
+        def project(start):
+            down[start] = dot(hidden[t, start : start + GROUP, :], wd[k], (1, 1))
+
+        def finish(start):
             for r in range(GROUP // SIDE):
-                y = first[pl.ds(start + r * SIDE, SIDE), :] + down[r * SIDE : r * SIDE + SIDE] + d_bias
-                ybuf[z, i + r] = y.astype(BF16)
-            return carry
-        groups(rest, 0)
+                part = slice(start + r * SIDE, start + r * SIDE + SIDE)
+                y = first[part, :] + down[start][r * SIDE : r * SIDE + SIDE] + d_bias
+                ybuf[z, start // SIDE + r] = y.astype(BF16)
+
+        in_turn([mix, layer_norm, activate, project, finish], starts)
 
         @pl.when(k == 0)
         def _():
@@ -382,11 +401,12 @@
             acc_d[k, n] += dot(gbt[...], hidden[t, :, n * WIDE : n * WIDE + WIDE])
         tick(1)
 
-        def chain(start, acc):
-            rows = pl.ds(start, GROUP)
-            x_acc, n_acc, m_acc, u_acc = acc
-            u_acc = list(u_acc)
-            low = gb[rows, :]
+        starts = [g * GROUP for g in range(ROWS // GROUP)]
+        sums = {"x": zero, "n": zero, "m": zero, "u": [jnp.zeros((8, FT), F32) for _ in range(FF // FT)]}
+        kept = {}
+
+        def through_gelu(start):
+            low = gb[start : start + GROUP, :]
             raw = dot(low, wd[k, :, 0:FT])
             for n in range(FF // FT):
                 cols = slice(n * FT, n * FT + FT)
@@ -394,14 +414,18 @@
                 if n + 1 < FF // FT:
                     raw = dot(low, wd[k, :, n * FT + FT : n * FT + 2 * FT])
                 for o in range(0, GROUP, TILE):
-                    part = pl.ds(start + o, TILE)
+                    part = slice(start + o, start + o + TILE)
                     gpn = (now[o : o + TILE] * gp[t, part, cols].astype(F32)).astype(BF16)
                     gpre[part, cols] = gpn
-                    u_acc[n] = u_acc[n] + fold(gpn.astype(F32))
-            back = dot(gpre[rows, :], wu[k], (1, 1))
+                    sums["u"][n] = sums["u"][n] + fold(gpn.astype(F32))
+
+        def through_up(start):
+            kept["back", start] = dot(gpre[start : start + GROUP, :], wu[k], (1, 1))
+
+        def through_norm(start):
             for o in range(0, GROUP, TILE):
-                part = pl.ds(start + o, TILE)
-                g = back[o : o + TILE]
+                part = slice(start + o, start + o + TILE)
+                g = kept["back", start][o : o + TILE]
                 x = xl[t, part, :].astype(F32)
                 gn = g * n_gain
                 mean_g = jnp.mean(gn, 1, keepdims=True)
@@ -410,44 +434,50 @@
                 gf[t, part, :] = out
                 low = out.astype(BF16)
                 gmb[part, :] = low
-                x_acc = x_acc + fold(g * x)
-                n_acc = n_acc + fold(g)
-                m_acc = m_acc + fold(low.astype(F32))
-            low = gmb[rows, :]
-            g_w = dot(low, wm[k, :, 0:C])
-            g_h = dot(low, wmid[k])
+                sums["x"] = sums["x"] + fold(g * x)
+                sums["n"] = sums["n"] + fold(g)
+                sums["m"] = sums["m"] + fold(low.astype(F32))
+
+        def through_merge(start):
+            low = gmb[start : start + GROUP, :]
+            kept["w", start] = dot(low, wm[k, :, 0:C])
+            kept["h", start] = dot(low, wmid[k])
+            kept["third", start] = dot(low, wm[k, :, 2 * C : 3 * C])
+
+        def round_branches(start):
             for o in range(0, GROUP, TILE):
-                part = pl.ds(start + o, TILE)
-                one = g_w[o : o + TILE].astype(BF16)
-                gwb[o : o + TILE, :] = one
+                part = slice(start + o, start + o + TILE)
+                one = kept["w", start][o : o + TILE].astype(BF16)
+                gwb[part, :] = one
                 wcol[part, :] += jnp.sum(one.astype(F32), 1, keepdims=True)
-                one = g_h[o : o + TILE].astype(BF16)
+                one = kept["h", start][o : o + TILE].astype(BF16)
                 gwh[part, :] = one
                 hcol[part, :] += jnp.sum(one.astype(F32), 1, keepdims=True)
-            third = dot(low, wm[k, :, 2 * C : 3 * C])
-            crossed = dot(kw[...], gwb[...])
+
+        def across_width(start):
+            rows = slice(start, start + GROUP)
+            crossed = dot(kw[...], gwb[rows, :])
             for o in range(0, GROUP, TILE):
-                gmix[t, pl.ds(start + o, TILE), :] = third[o : o + TILE] + crossed[o : o + TILE]
-            gw_acc[...] += dot(gwb[...], joined[t, rows, 2 * C : 3 * C], (1, 1))
-            return (x_acc, n_acc, m_acc, u_acc)
-        acc = groups(chain, (zero, zero, zero, [jnp.zeros((8, FT), F32) for _ in range(FF // FT)]))
+                part = slice(start + o, start + o + TILE)
+                gmix[t, part, :] = kept["third", start][o : o + TILE] + crossed[o : o + TILE]
+            gw_acc[...] += dot(gwb[rows, :], joined[t, rows, 2 * C : 3 * C], (1, 1))
+
+        in_turn([through_gelu, through_up, through_norm, through_merge, round_branches, across_width], starts)
+        gs[k, NGAIN : NGAIN + 1, :] += total(sums["x"])
+        gs[k, NBIAS : NBIAS + 1, :] += total(sums["n"])
+        gs[k, MBIAS : MBIAS + 1, :] += total(sums["m"])
+        for n in range(FF // FT):
+            gs[k, UBIAS + n : UBIAS + n + 1, 0:FT] += total(sums["u"][n])
         tick(4)
-        gs[k, NGAIN : NGAIN + 1, :] += total(acc[0])
-        gs[k, NBIAS : NBIAS + 1, :] += total(acc[1])
-        gs[k, MBIAS : MBIAS + 1, :] += total(acc[2])
-        for n in range(FF // FT):
-            gs[k, UBIAS + n : UBIAS + n + 1, 0:FT] += total(acc[3][n])
         gbt[...] = normal[t].T
         for n in range(2):
             acc_u[k, n] += dot(gbt[...], gpre[:, n * WIDE : n * WIDE + WIDE])
-        tick(5)
-        gbt[...] = gmb[...].T
+        gmt[...] = gmb[...].T
         for n in range(2):
             width = min(MT, 3 * C - n * MT)
-            acc_m[k, n, :, 0:width] += dot(gbt[...], joined[t, :, n * MT : n * MT + width])
+            acc_m[k, n, :, 0:width] += dot(gmt[...], joined[t, :, n * MT : n * MT + width])
         tick(6)
         gh_acc[...] += dot(gwh[...], joined[t, :, 2 * C : 3 * C], (1, 1))
-        tick(10)
 
         def batch_sums(start, acc):
             plain, cross = acc
@@ -698,7 +728,7 @@
     taps_sum = small_sum(slice(0, SMALL), conv_land, conv_send, conv_recv)
 
     plan = {}
-    backward_places, input_places = [0, 1, 4, 5, 6, 10, 11], [7, 8, 9]
+    backward_places, input_places = [0, 1, 4, 6, 11], [7, 8, 9]
     order = []
     for n in range(6):
         order += [(n, p) for p in input_places] if n > 1 else []
@@ -712,9 +742,9 @@
             at += gap
         return steps
 
-    for which, place in enumerate((1, 5, 6)):
-        assert not put((1, place), reduction(1, which), 2 if n_swaps < 3 else 1)
-    tails = [put((3, place), reduction(0, which), 1) for which, place in enumerate((1, 5, 6))]
+    for which, place in enumerate((1, 6, 6)):
+        assert not put((1, place), reduction(1, which), 1)
+    tails = [put((3, place), reduction(0, which), 1) for which, place in enumerate((1, 6, 6))]
     tails.append(put((4, 7), small, 1))
     tails.append(list(taps_sum))
 
@@ -927,7 +957,8 @@
             pltpu.VMEM((2, ROWS, C), F32),
             pltpu.VMEM((ROWS, C), BF16),
             pltpu.VMEM((ROWS, C), BF16),
-            pltpu.VMEM((GROUP, C), BF16),
+            pltpu.VMEM((ROWS, C), BF16),
+            pltpu.VMEM((C, ROWS), BF16),
             pltpu.VMEM((C, ROWS), BF16),
             pltpu.VMEM((ROWS, FF), BF16),
             pltpu.VMEM((2, ROWS, C), F32),

time: 180 us -> 164 us (0.911)
  Pallas kernels: 179 us -> 163 us
    pallas_call x1, Pallas kernels: 172 us -> 157 us  [on_device(): pl.pallas_call(functools.partial(kernel, n_dp), out_shape=(shape((1, micr...]
where the time goes in v1:
time: 164 us
  Pallas kernels  163 us (99%)
    pallas_call x1, Pallas kernels, on_device(): pl.pallas_call(functools.partial(kernel, n_dp), out_shape=(shape((1, micr...  157 us
    pallas_call x1, Pallas kernels, on_device(): pl.pallas_call(finish_kernel, out_shape=(shape((1, micro) + grid, BF16),...  6.75 us

profile of v1, /device:TPU:0, one launch (start us, length us, event | category | flops | bytes accessed | tf_op | source)
XLA Modules:
  0.0 164.3 jit_solution(2383995133849317001)
XLA Ops:
  0.7 156.7 %shard_map.305 = (bf16[1,4,24,24,320]{4,3,2,1,0:T(8,128)(2,1)}, bf16[1,4,24,24,320]{4,3,2,1,0:T(8,128)(2,1)}, bf16[2,4,80,640]{3,2,1,0:T(8,128)(2,1)}, bf16[2,4,...) custom-call(bf16[4,24,24,320]{3,2,1,0:T(8,128)(2,1)} %images.1, ...), custom_call_target="tpu_custom_call" | custom-call | tf_op jit(solution)/shard_map/pallas_call | solution.py:921
  157.4 6.7 %shard_map.306 = (bf16[1,4,24,24,320]{4,3,2,1,0:T(8,128)(2,1)}, bf16[1,4,24,24,320]{4,3,2,1,0:T(8,128)(2,1)}, f32[9,1,320]{2,1,0:T(1,128)}, f32[1,320]{1,0:T(1,1...) custom-call(bf16[1,4,24,24,320]{4,3,2,1,0:T(8,128)(2,1)} %get-tuple-, ...), custom_call_target="tpu_custom_call" | custom-call | tf_op jit(solution)/shard_map/pallas_call | solution.py:1006

commit v2 on v1

--- a/solution.py
+++ b/solution.py
@@ -72,7 +72,6 @@
     e = jnp.exp2(x * x * -0.7213475204444817)
     d = 1.0 + 0.23164189 * jnp.abs(x)
     t = pl.reciprocal(d, approx=True)
-    t = t * (2.0 - d * t)
     poly = t * (0.127414796 + t * (-0.142248368 + t * (0.7107068705 + t * (-0.7265760135 + t * 0.5307027145))))
     tail = poly * e
     phi = jnp.where(x >= 0, 1.0 - tail, tail)
@@ -462,20 +461,27 @@
                 gmix[t, part, :] = kept["third", start][o : o + TILE] + crossed[o : o + TILE]
             gw_acc[...] += dot(gwb[rows, :], joined[t, rows, 2 * C : 3 * C], (1, 1))
 
-        in_turn([through_gelu, through_up, through_norm, through_merge, round_branches, across_width], starts)
+        def up_grad(start):
+            if start == starts[-1]:
+                gbt[...] = normal[t].T
+                for n in range(2):
+                    acc_u[k, n] += dot(gbt[...], gpre[:, n * WIDE : n * WIDE + WIDE])
+
+        def merge_grad(start):
+            if start == starts[-1]:
+                gmt[...] = gmb[...].T
+                for n in range(2):
+                    width = min(MT, 3 * C - n * MT)
+                    acc_m[k, n, :, 0:width] += dot(gmt[...], joined[t, :, n * MT : n * MT + width])
+
+        in_turn([
+            through_gelu, through_up, up_grad, through_norm, through_merge, merge_grad, round_branches, across_width,
+        ], starts)
         gs[k, NGAIN : NGAIN + 1, :] += total(sums["x"])
         gs[k, NBIAS : NBIAS + 1, :] += total(sums["n"])
         gs[k, MBIAS : MBIAS + 1, :] += total(sums["m"])
         for n in range(FF // FT):
             gs[k, UBIAS + n : UBIAS + n + 1, 0:FT] += total(sums["u"][n])
-        tick(4)
-        gbt[...] = normal[t].T
-        for n in range(2):
-            acc_u[k, n] += dot(gbt[...], gpre[:, n * WIDE : n * WIDE + WIDE])
-        gmt[...] = gmb[...].T
-        for n in range(2):
-            width = min(MT, 3 * C - n * MT)
-            acc_m[k, n, :, 0:width] += dot(gmt[...], joined[t, :, n * MT : n * MT + width])
         tick(6)
         gh_acc[...] += dot(gwh[...], joined[t, :, 2 * C : 3 * C], (1, 1))
 
@@ -728,7 +734,7 @@
     taps_sum = small_sum(slice(0, SMALL), conv_land, conv_send, conv_recv)
 
     plan = {}
-    backward_places, input_places = [0, 1, 4, 6, 11], [7, 8, 9]
+    backward_places, input_places = [0, 1, 6, 11], [7, 8, 9]
     order = []
     for n in range(6):
         order += [(n, p) for p in input_places] if n > 1 else []
@@ -744,8 +750,8 @@
 
     for which, place in enumerate((1, 6, 6)):
         assert not put((1, place), reduction(1, which), 1)
-    tails = [put((3, place), reduction(0, which), 1) for which, place in enumerate((1, 6, 6))]
-    tails.append(put((4, 7), small, 1))
+    tails = [put((3, place), reduction(0, which), 2 if which else 1) for which, place in enumerate((1, 6, 6))]
+    tails.append(put((4, 7), small, 2))
     tails.append(list(taps_sum))
 
     pack_over.wait()

time: 164 us -> 165 us (level)
  no operation moved by 1% of the time
where the time goes in v2:
time: 165 us
  Pallas kernels  164 us (99%)
    pallas_call x1, Pallas kernels, on_device(): pl.pallas_call(functools.partial(kernel, n_dp), out_shape=(shape((1, micr...  157 us
    pallas_call x1, Pallas kernels, on_device(): pl.pallas_call(finish_kernel, out_shape=(shape((1, micro) + grid, BF16),...  6.75 us

profile of v2, /device:TPU:0, one launch (start us, length us, event | category | flops | bytes accessed | tf_op | source)
XLA Modules:
  0.0 164.7 jit_solution(11831087464507504707)
XLA Ops:
  0.7 157.1 %shard_map.305 = (bf16[1,4,24,24,320]{4,3,2,1,0:T(8,128)(2,1)}, bf16[1,4,24,24,320]{4,3,2,1,0:T(8,128)(2,1)}, bf16[2,4,80,640]{3,2,1,0:T(8,128)(2,1)}, bf16[2,4,...) custom-call(bf16[4,24,24,320]{3,2,1,0:T(8,128)(2,1)} %images.1, ...), custom_call_target="tpu_custom_call" | custom-call | tf_op jit(solution)/shard_map/pallas_call | solution.py:927
  157.8 6.7 %shard_map.306 = (bf16[1,4,24,24,320]{4,3,2,1,0:T(8,128)(2,1)}, bf16[1,4,24,24,320]{4,3,2,1,0:T(8,128)(2,1)}, f32[9,1,320]{2,1,0:T(1,128)}, f32[1,320]{1,0:T(1,1...) custom-call(bf16[1,4,24,24,320]{4,3,2,1,0:T(8,128)(2,1)} %get-tuple-, ...), custom_call_target="tpu_custom_call" | custom-call | tf_op jit(solution)/shard_map/pallas_call | solution.py:1012
